TPU v7x, 512 devices: a whole 4x4x16 slice. The times are simulated.
512 devices in a mesh: pm: 2 (over y_lo), ka: 128 (over x, z, core), isdf: 2 (over y_hi).
Axes of the slice: x: 4, y: 4 (y_hi: 2, y_lo: 2; y = y_hi * 2 + y_lo), z: 16, core: 2. Of those that a mesh axis runs over, the one named last changes fastest.
Arguments:
- amplitudes: bfloat16 [2, 2, 2, 256, 64, 256], P('pm', None, None, 'ka'), may hold values from -6 to 6
- conduction: bfloat16 [2, 256, 256, 512], P(None, 'ka', None, 'isdf'), may hold values from -0.375 to 0.375
- valence: bfloat16 [2, 256, 64, 512], P(None, 'ka'), may hold values from -0.75 to 0.75
- energy: float32 [256, 64, 256], P('ka', None, 'isdf'), may hold values from 0.5 to 2.5
- screened: bfloat16 [4, 2, 512, 512], P(None, None, 'isdf'), may hold values from -0.59765625 to 0.59765625
- coulomb: float32 [512, 512], P(None, 'isdf'), may hold values from -0.03125 to 0.03125
- mirror: int32 [256], P('ka'), may hold values from 0 to 255, as said below
- transfer_class: int32 [256, 256], P('ka'), may hold values from 0 to 3, as said below
Outputs:
- response: bfloat16 [2, 2, 2, 256, 64, 256], P('pm', None, None, 'ka', None, 'isdf')
Inputs may be any that keep to these rules, and one draw needn't show every extreme that they name: mirror[mirror[k]] = k; a k-point of block j (the aligned block of 2 k-points that holds it) has its mirror in block 127 - j. transfer_class[k, k2] depends only on (k - k2) mod 256.
All inputs are finite; a program needn't handle non-finite values.
Results may differ from a plain program's by a relative error of at most 0.015.
Values may be sent and summed in bfloat16 or wider, within the bound.
A program may use at most 128 MiB of HBM per device.

v0:
```python
import jax
import jax.numpy as jnp
from jax import lax
from jax.sharding import PartitionSpec as P

REACH = 2
HIGHEST = lax.Precision.HIGHEST


def swapped(block, axis, apart):
    count = lax.axis_size(axis)
    route = []
    for low in range(count):
        high = low | 1 << apart
        if high != low and high < count:
            route += [(low, high), (high, low)]
    return lax.ppermute(block, axis, route)


def shifted(value, axis, by):
    size = lax.axis_size(axis)
    return lax.ppermute(value, axis, [(i, (i + by) % size) for i in range(size)])


def pair_einsum(pattern, left, right, conjugate):

    def single(first, second):
        return jnp.einsum(pattern, first, second, preferred_element_type=jnp.float32)

    if conjugate:
        real_part = single(left[0], right[0]) + single(left[1], right[1])
        imag_part = single(left[1], right[0]) - single(left[0], right[1])
    else:
        real_part = single(left[0], right[0]) - single(left[1], right[1])
        imag_part = single(left[0], right[1]) + single(left[1], right[0])
    return (real_part, imag_part)


def conjugated(field):
    return jnp.stack([field[:, 0], -field[:, 1]], axis=1)


def coefficients(vector, conduction):
    real_part, imag_part = pair_einsum(
        "bkvc,kcm->bkvm", (vector[:, 0], vector[:, 1]), (conduction[0], conduction[1]), False
    )
    return jnp.stack([real_part, imag_part], axis=1).astype(jnp.bfloat16)


def amp_bits(field):
    for bit_number in range(lax.axis_size("ka").bit_length() - 1):
        field = swapped(field, "ka", bit_number)
    return field


def result_bits(field):
    for bit_number in range(lax.axis_size("ka").bit_length() - 1):
        field = swapped(field, "ka", bit_number)
    return field


def by_mirror(field, local_mirror):
    index = local_mirror[None, None, :, None, None]
    return jnp.where(index == 0, field[:, :, 0:1], field[:, :, 1:2])


def per_device(amplitudes, conduction, valence, energy, screened, coulomb, mirror, transfer_class):
    pm_index = lax.axis_index("pm")
    ka_index = lax.axis_index("ka")
    isdf_index = lax.axis_index("isdf")
    ka_count = lax.axis_size("ka")
    kpoint_count = conduction.shape[1]
    mu_count = conduction.shape[3]
    point_count = valence.shape[3]
    cond_share = energy.shape[2]
    vector_count = amplitudes.shape[1]
    is_plus = pm_index == 0
    parity = jnp.where(is_plus, 1.0, -1.0).astype(jnp.float32)
    exchange_weight = jnp.where(is_plus, 4.0, 0.0).astype(jnp.float32)
    local_amps = amplitudes[0]
    partner_amps = swapped(local_amps, "pm", 0)
    partner_side = jnp.where(is_plus, partner_amps, local_amps)
    distant_side = amp_bits(partner_side)
    direct = jnp.where(is_plus, local_amps, partner_amps).astype(jnp.float32)
    local_mirror = mirror - (ka_count - 1 - ka_index) * kpoint_count
    flipped = conjugated(by_mirror(distant_side, local_mirror).astype(jnp.float32))
    vector = (direct + parity * flipped).astype(jnp.bfloat16)
    own_coef = coefficients(vector, conduction)
    valence_part = lax.dynamic_slice_in_dim(valence, isdf_index * mu_count, mu_count, 3)
    rho_real = jnp.einsum(
        "kvm,bkvm->bm", valence_part[0], own_coef[:, 0], preferred_element_type=jnp.float32
    )
    rho_real = rho_real + jnp.einsum(
        "kvm,bkvm->bm", valence_part[1], own_coef[:, 1], preferred_element_type=jnp.float32
    )
    rho_imag = jnp.einsum(
        "kvm,bkvm->bm", valence_part[0], own_coef[:, 1], preferred_element_type=jnp.float32
    )
    rho_imag = rho_imag - jnp.einsum(
        "kvm,bkvm->bm", valence_part[1], own_coef[:, 0], preferred_element_type=jnp.float32
    )
    density = jnp.stack([rho_real, rho_imag], axis=1)
    spread = jnp.einsum("nm,brm->brn", coulomb, density, precision=HIGHEST)
    spread = lax.psum(spread, ("ka", "isdf"))
    potential = lax.dynamic_slice_in_dim(spread, isdf_index * mu_count, mu_count, 2)
    class_ids = jnp.arange(screened.shape[0], dtype=jnp.int32)

    def accumulate(totals, coef_block, valence_block, source):
        pair_real, pair_imag = pair_einsum(
            "bqvm,qvn->bqmn",
            (coef_block[:, 0], coef_block[:, 1]),
            (valence_block[0], valence_block[1]),
            True,
        )
        pair_real = pair_real.astype(jnp.bfloat16)
        pair_imag = pair_imag.astype(jnp.bfloat16)
        classes = lax.dynamic_slice_in_dim(transfer_class, source * kpoint_count, kpoint_count, 1)
        selector = (classes[:, :, None] == class_ids).astype(jnp.bfloat16)
        total_real, total_imag = totals
        for visitor in range(kpoint_count):
            chosen = jnp.einsum(
                "kw,wrmn->rkmn", selector[:, visitor], screened, preferred_element_type=jnp.float32
            ).astype(jnp.bfloat16)
            screen_real = chosen[0][None].astype(jnp.float32)
            screen_imag = chosen[1][None].astype(jnp.float32)
            visit_real = pair_real[:, visitor][:, None].astype(jnp.float32)
            visit_imag = pair_imag[:, visitor][:, None].astype(jnp.float32)
            total_real = total_real + (screen_real * visit_real - screen_imag * visit_imag)
            total_imag = total_imag + (screen_real * visit_imag + screen_imag * visit_real)
        return (total_real, total_imag)

    payload = (vector, conduction, valence)

    def advance(moving, offset):
        return shifted((moving[0], moving[1], moving[2]), "ka", offset)

    def unpack(moving):
        return (coefficients(moving[0], moving[1]), moving[2])

    def visit(totals, moving, distance):
        coef_block, valence_block = unpack(moving)
        source = jnp.mod(ka_index + distance, ka_count)
        return accumulate(totals, coef_block, valence_block, source)

    zero_field = jnp.zeros((vector_count, kpoint_count, mu_count, point_count), jnp.float32)
    totals = accumulate((zero_field, zero_field), own_coef, valence, ka_index)
    below_item = payload
    for count_done in range(REACH):
        below_item = advance(below_item, 1)
        totals = visit(totals, below_item, -(count_done + 1))
    above_item = payload
    for count_done in range(REACH):
        above_item = advance(above_item, -1)
        totals = visit(totals, above_item, count_done + 1)
    sum_real = totals[0].astype(jnp.bfloat16)
    sum_imag = totals[1].astype(jnp.bfloat16)
    back_real, back_imag = pair_einsum(
        "bkmn,kvn->bkvm", (sum_real, sum_imag), (valence[0], valence[1]), False
    )
    potential_real = potential[:, 0][:, None, None, :]
    potential_imag = potential[:, 1][:, None, None, :]
    exchange_real = potential_real * valence_part[0] - potential_imag * valence_part[1]
    exchange_imag = potential_real * valence_part[1] + potential_imag * valence_part[0]
    field_real = (exchange_weight * exchange_real - back_real).astype(jnp.bfloat16)
    field_imag = (exchange_weight * exchange_imag - back_imag).astype(jnp.bfloat16)
    out_real, out_imag = pair_einsum(
        "bkvm,kcm->bkvc", (field_real, field_imag), (conduction[0], conduction[1]), True
    )
    partial_out = jnp.stack([out_real, out_imag], axis=1)
    summed = lax.psum_scatter(
        partial_out.astype(jnp.bfloat16), "isdf", scatter_dimension=4, tiled=True
    ).astype(jnp.float32)
    vector_part = lax.dynamic_slice_in_dim(vector, isdf_index * cond_share, cond_share, 4).astype(
        jnp.float32
    )
    channel_out = (energy[None, None] * vector_part + summed).astype(jnp.bfloat16)
    partner_out = swapped(channel_out, "pm", 0)
    blended = (
        0.5 * (partner_out.astype(jnp.float32) + parity * channel_out.astype(jnp.float32))
    ).astype(jnp.bfloat16)
    distant_out = result_bits(blended)
    reflected = conjugated(by_mirror(distant_out, local_mirror))
    result = jnp.where(is_plus, blended, reflected)
    return result[None]


def solution(mesh):
    return jax.shard_map(
        per_device,
        mesh=mesh,
        in_specs=(
            P("pm", None, None, "ka", None, None),
            P(None, "ka", None, "isdf"),
            P(None, "ka", None, None),
            P("ka", None, "isdf"),
            P(None, None, "isdf", None),
            P(None, "isdf"),
            P("ka"),
            P("ka", None),
        ),
        out_specs=P("pm", None, None, "ka", None, "isdf"),
        check_vma=False,
    )
```

profile of v0, /device:TPU:2, one launch (start us, length us, event | category | flops | bytes accessed | tf_op | source)
XLA Modules:
  0.0 1086.2 jit_solution(11353441118219177994)
XLA Ops:
  8.6 10.8 collective-permute-start.15
  21.3 5.8 collective-permute-start.16
  78.0 6.5 collective-permute-done.2
  88.5 12.3 %collective-permute-done.3 = bf16[2,2,2,64,256]{4,3,0,2,1:T(8,128)(2,1)S(1)} collective-permute-done((bf16[2,2,2,64,256]{4,3,0,2,1:T(8,128)(2,1)S(1)}, bf16[2,2,2,64,256]{4,3,0,2,1:T(8,128)(2,1)S(1)}, u32[]{:S(2)}, u32[]{:S(2)}) %collective-permute-start.3) | collective-permute-done | bytes 262176 | tf_op jit(solution)/shard_map/ppermute | solution.py:17
  105.3 22.7 %collective-permute-done.4 = bf16[2,2,2,64,256]{4,3,0,2,1:T(8,128)(2,1)S(1)} collective-permute-done((bf16[2,2,2,64,256]{4,3,0,2,1:T(8,128)(2,1)S(1)}, bf16[2,2,2,64,256]{4,3,0,2,1:T(8,128)(2,1)S(1)}, u32[]{:S(2)}, u32[]{:S(2)}) %collective-permute-start.4) | collective-permute-done | bytes 262176 | tf_op jit(solution)/shard_map/ppermute | solution.py:17
  128.0 14.7 %collective-permute-start.5 = (bf16[2,2,2,64,256]{4,3,0,2,1:T(8,128)(2,1)S(1)}, bf16[2,2,2,64,256]{4,3,0,2,1:T(8,128)(2,1)S(1)}, u32[]{:S(2)}, u32[]{:S(2)}) collective-permute-start(bf16[2,2,2,64,256]{4,3,0,2,1:T(8,128)(2,1)S(1)} %collective-permute-done.4), channel_id=1, source_target_pairs={{0,32},{32,0},{2,34},{34,2},{4,36},{36,4},{6,38},{38,6},{8,40},{40... | collective-permute-start | bytes 786440 | tf_op jit(solution)/shard_map/ppermute | solution.py:17
  144.7 14.9 %collective-permute-done.5 = bf16[2,2,2,64,256]{4,3,0,2,1:T(8,128)(2,1)S(1)} collective-permute-done((bf16[2,2,2,64,256]{4,3,0,2,1:T(8,128)(2,1)S(1)}, bf16[2,2,2,64,256]{4,3,0,2,1:T(8,128)(2,1)S(1)}, u32[]{:S(2)}, u32[]{:S(2)}) %collective-permute-start.5) | collective-permute-done | bytes 262176 | tf_op jit(solution)/shard_map/ppermute | solution.py:17
  164.4 5.4 collective-permute-done.6
  200.1 5.8 collective-permute-start.19
  207.9 5.8 collective-permute-start.18
  225.0 583.0 %psum.7 = f32[2,2,512]{2,1,0:T(2,128)S(1)} all-reduce(f32[2,2,512]{2,1,0:T(2,128)S(1)} %fusion.90), channel_id=1, replica_groups=mesh['pm'=2,'ka'=128,'isdf'=2] {'ka','isdf'}, use_global_device_ids=true, to_apply=%region_0.1 | all-reduce | flops 2048 | bytes 16384 | tf_op jit(solution)/shard_map/psum | solution.py:104
  842.2 5.3 collective-permute-start.17
  875.2 9.2 add_convert_fusion
  884.5 9.5 add_convert_fusion.1
  898.4 92.4 %reduce-scatter.4.cloned.1.call-done = bf16[128,512]{1,0:T(8,128)(2,1)} async-done(((bf16[256,512]{1,0:T(8,128)(2,1)}), bf16[128,512]{1,0:T(8,128)(2,1)}) %reduce-scatter.4.cloned.1.call-update) | async-done | bytes 131088
  995.6 4.6 collective-permute-done.20
  1011.0 4.4 collective-permute-start.23
  1015.4 5.9 collective-permute-done.23
  1021.3 7.6 collective-permute-start.24
  1028.9 9.8 collective-permute-done.24
  1038.7 12.0 %collective-permute-start.25 = (bf16[2,2,2,64,128]{4,3,0,2,1:T(8,128)(2,1)S(1)}, bf16[2,2,2,64,128]{4,3,0,2,1:T(8,128)(2,1)S(1)}, u32[]{:S(2)}, u32[]{:S(2)}) collective-permute-start(bf16[2,2,2,64,128]{4,3,0,2,1:T(8,128)(2,1)S(1)} %collective-permute-done.24), channel_id=1, source_target_pairs={{0,32},{32,0},{2,34},{34,2},{4,36},{36,4},{6,38},{38,6},{8,40},{40... | collective-permute-start | bytes 393224 | tf_op jit(solution)/shard_map/ppermute | solution.py:17
  1050.8 12.1 %collective-permute-done.25 = bf16[2,2,2,64,128]{4,3,0,2,1:T(8,128)(2,1)S(1)} collective-permute-done((bf16[2,2,2,64,128]{4,3,0,2,1:T(8,128)(2,1)S(1)}, bf16[2,2,2,64,128]{4,3,0,2,1:T(8,128)(2,1)S(1)}, u32[]{:S(2)}, u32[]{:S(2)}) %collective-permute-start.25) | collective-permute-done | bytes 131104 | tf_op jit(solution)/shard_map/ppermute | solution.py:17
  1065.3 4.4 collective-permute-done.26
  1073.7 4.4 collective-permute-done.27
  (292 shorter events, 201.8 us)
Async XLA Ops:
  6.5 984.3 %reduce-scatter.4.cloned.1.call-start = ((), (), s32[]{:S(2)}) async-start(), calls=%async_computation.1 | async-start | bytes 393216
  6.5 199.4 %collective-permute-start.9 = (bf16[2,2,256,256]{3,2,1,0:T(8,128)(2,1)}, bf16[2,2,256,256]{3,2,1,0:T(8,128)(2,1)}, u32[]{:S(2)}, u32[]{:S(2)}) collective-permute-start(bf16[2,2,256,256]{3,2,1,0:T(8,128)(2,1)} %param.9), channel_id=1, source_target_pairs={{0,2},{2,4},{4,6},{6,8},{8,10},{10,12},{12,14},{14,16},{16,18},{18... | collective-permute-start | bytes 1572872 | tf_op jit(solution)/shard_map/ppermute | solution.py:22
  8.6 199.3 %collective-permute-start.15 = (bf16[2,2,256,256]{3,2,1,0:T(8,128)(2,1)}, bf16[2,2,256,256]{3,2,1,0:T(8,128)(2,1)}, u32[]{:S(2)}, u32[]{:S(2)}) collective-permute-start(bf16[2,2,256,256]{3,2,1,0:T(8,128)(2,1)} %param.9), channel_id=1, source_target_pairs={{0,254},{2,0},{4,2},{6,4},{8,6},{10,8},{12,10},{14,12},{16,14},{18... | collective-permute-start | bytes 1572872 | tf_op jit(solution)/shard_map/ppermute | solution.py:22
  19.4 178.6 %collective-permute-start.10 = (bf16[2,2,64,512]{3,2,1,0:T(8,128)(2,1)}, bf16[2,2,64,512]{3,2,1,0:T(8,128)(2,1)}, u32[]{:S(2)}, u32[]{:S(2)}) collective-permute-start(bf16[2,2,64,512]{3,2,1,0:T(8,128)(2,1)} %param.10), channel_id=1, source_target_pairs={{0,2},{2,4},{4,6},{6,8},{8,10},{10,12},{12,14},{14,16},{16,18},{18... | collective-permute-start | bytes 786440 | tf_op jit(solution)/shard_map/ppermute | solution.py:22
  21.3 178.8 %collective-permute-start.16 = (bf16[2,2,64,512]{3,2,1,0:T(8,128)(2,1)}, bf16[2,2,64,512]{3,2,1,0:T(8,128)(2,1)}, u32[]{:S(2)}, u32[]{:S(2)}) collective-permute-start(bf16[2,2,64,512]{3,2,1,0:T(8,128)(2,1)} %param.10), channel_id=1, source_target_pairs={{0,254},{2,0},{4,2},{6,4},{8,6},{10,8},{12,10},{14,12},{16,14},{18... | collective-permute-start | bytes 786440 | tf_op jit(solution)/shard_map/ppermute | solution.py:22
  28.1 41.6 %collective-permute-start = (bf16[2,2,2,64,256]{4,3,0,2,1:T(8,128)(2,1)S(1)}, bf16[2,2,2,64,256]{4,3,0,2,1:T(8,128)(2,1)S(1)}, u32[]{:S(2)}, u32[]{:S(2)}) collective-permute-start(bf16[2,2,2,64,256]{4,3,0,2,1:T(8,128)(2,1)S(1)} %bitcast.655), channel_id=1, source_target_pairs={{0,256},{256,0},{1,257},{257,1},{2,258},{258,2},{3,259},{259,3},{4... | collective-permute-start | bytes 786440 | tf_op jit(solution)/shard_map/ppermute | solution.py:17
  73.9 10.7 collective-permute-start.2
  84.6 16.3 %collective-permute-start.3 = (bf16[2,2,2,64,256]{4,3,0,2,1:T(8,128)(2,1)S(1)}, bf16[2,2,2,64,256]{4,3,0,2,1:T(8,128)(2,1)S(1)}, u32[]{:S(2)}, u32[]{:S(2)}) collective-permute-start(bf16[2,2,2,64,256]{4,3,0,2,1:T(8,128)(2,1)S(1)} %collective-permute-done.2), channel_id=1, source_target_pairs={{0,8},{8,0},{2,10},{10,2},{4,12},{12,4},{6,14},{14,6},{16,24},{24,... | collective-permute-start | bytes 786440 | tf_op jit(solution)/shard_map/ppermute | solution.py:17
  100.8 27.1 %collective-permute-start.4 = (bf16[2,2,2,64,256]{4,3,0,2,1:T(8,128)(2,1)S(1)}, bf16[2,2,2,64,256]{4,3,0,2,1:T(8,128)(2,1)S(1)}, u32[]{:S(2)}, u32[]{:S(2)}) collective-permute-start(bf16[2,2,2,64,256]{4,3,0,2,1:T(8,128)(2,1)S(1)} %collective-permute-done.3), channel_id=1, source_target_pairs={{0,16},{16,0},{2,18},{18,2},{4,20},{20,4},{6,22},{22,6},{8,24},{24... | collective-permute-start | bytes 786440 | tf_op jit(solution)/shard_map/ppermute | solution.py:17
  128.0 31.6 %collective-permute-start.5 = (bf16[2,2,2,64,256]{4,3,0,2,1:T(8,128)(2,1)S(1)}, bf16[2,2,2,64,256]{4,3,0,2,1:T(8,128)(2,1)S(1)}, u32[]{:S(2)}, u32[]{:S(2)}) collective-permute-start(bf16[2,2,2,64,256]{4,3,0,2,1:T(8,128)(2,1)S(1)} %collective-permute-done.4), channel_id=1, source_target_pairs={{0,32},{32,0},{2,34},{34,2},{4,36},{36,4},{6,38},{38,6},{8,40},{40... | collective-permute-start | bytes 786440 | tf_op jit(solution)/shard_map/ppermute | solution.py:17
  159.6 10.2 collective-permute-start.6
  169.8 43.8 %collective-permute-start.7 = (bf16[2,2,2,64,256]{4,3,0,2,1:T(8,128)(2,1)}, bf16[2,2,2,64,256]{4,3,0,2,1:T(8,128)(2,1)}, u32[]{:S(2)}, u32[]{:S(2)}) collective-permute-start(bf16[2,2,2,64,256]{4,3,0,2,1:T(8,128)(2,1)} %collective-permute-done.6), channel_id=1, source_target_pairs={{0,128},{128,0},{2,130},{130,2},{4,132},{132,4},{6,134},{134,6},{8... | collective-permute-start | bytes 786440 | tf_op jit(solution)/shard_map/ppermute | solution.py:17
  198.1 654.0 %collective-permute-start.13 = (bf16[2,2,64,512]{3,2,1,0:T(8,128)(2,1)}, bf16[2,2,64,512]{3,2,1,0:T(8,128)(2,1)}, u32[]{:S(2)}, u32[]{:S(2)}) collective-permute-start(bf16[2,2,64,512]{3,2,1,0:T(8,128)(2,1)} %collective-permute-done.10), channel_id=1, source_target_pairs={{0,2},{2,4},{4,6},{6,8},{8,10},{10,12},{12,14},{14,16},{16,18},{18... | collective-permute-start | bytes 786440 | tf_op jit(solution)/shard_map/ppermute | solution.py:22
  200.1 664.4 %collective-permute-start.19 = (bf16[2,2,64,512]{3,2,1,0:T(8,128)(2,1)}, bf16[2,2,64,512]{3,2,1,0:T(8,128)(2,1)}, u32[]{:S(2)}, u32[]{:S(2)}) collective-permute-start(bf16[2,2,64,512]{3,2,1,0:T(8,128)(2,1)} %collective-permute-done.16), channel_id=1, source_target_pairs={{0,254},{2,0},{4,2},{6,4},{8,6},{10,8},{12,10},{14,12},{16,14},{18... | collective-permute-start | bytes 786440 | tf_op jit(solution)/shard_map/ppermute | solution.py:22
  205.9 636.3 %collective-permute-start.12 = (bf16[2,2,256,256]{3,2,1,0:T(8,128)(2,1)}, bf16[2,2,256,256]{3,2,1,0:T(8,128)(2,1)}, u32[]{:S(2)}, u32[]{:S(2)}) collective-permute-start(bf16[2,2,256,256]{3,2,1,0:T(8,128)(2,1)} %collective-permute-done.9), channel_id=1, source_target_pairs={{0,2},{2,4},{4,6},{6,8},{8,10},{10,12},{12,14},{14,16},{16,18},{18... | collective-permute-start | bytes 1572872 | tf_op jit(solution)/shard_map/ppermute | solution.py:22
  207.9 652.0 %collective-permute-start.18 = (bf16[2,2,256,256]{3,2,1,0:T(8,128)(2,1)}, bf16[2,2,256,256]{3,2,1,0:T(8,128)(2,1)}, u32[]{:S(2)}, u32[]{:S(2)}) collective-permute-start(bf16[2,2,256,256]{3,2,1,0:T(8,128)(2,1)} %collective-permute-done.15), channel_id=1, source_target_pairs={{0,254},{2,0},{4,2},{6,4},{8,6},{10,8},{12,10},{14,12},{16,14},{18... | collective-permute-start | bytes 1572872 | tf_op jit(solution)/shard_map/ppermute | solution.py:22
  217.9 594.7 %collective-permute-start.8 = (bf16[2,2,2,64,256]{4,3,0,2,1:T(8,128)(2,1)}, bf16[2,2,2,64,256]{4,3,0,2,1:T(8,128)(2,1)}, u32[]{:S(2)}, u32[]{:S(2)}) collective-permute-start(bf16[2,2,2,64,256]{4,3,0,2,1:T(8,128)(2,1)} %fusion.89), channel_id=1, source_target_pairs={{0,2},{2,4},{4,6},{6,8},{8,10},{10,12},{12,14},{14,16},{16,18},{18... | collective-permute-start | bytes 786440 | tf_op jit(solution)/shard_map/ppermute | solution.py:22
  812.6 14.6 %collective-permute-start.14 = (bf16[2,2,2,64,256]{4,3,0,2,1:T(8,128)(2,1)}, bf16[2,2,2,64,256]{4,3,0,2,1:T(8,128)(2,1)S(1)}, u32[]{:S(2)}, u32[]{:S(2)}) collective-permute-start(bf16[2,2,2,64,256]{4,3,0,2,1:T(8,128)(2,1)} %fusion.89), channel_id=1, source_target_pairs={{0,254},{2,0},{4,2},{6,4},{8,6},{10,8},{12,10},{14,12},{16,14},{18... | collective-permute-start | bytes 786440 | tf_op jit(solution)/shard_map/ppermute | solution.py:22
  827.2 20.3 %collective-permute-start.11 = (bf16[2,2,2,64,256]{4,3,0,2,1:T(8,128)(2,1)}, bf16[2,2,2,64,256]{4,3,0,2,1:T(8,128)(2,1)S(1)}, u32[]{:S(2)}, u32[]{:S(2)}) collective-permute-start(bf16[2,2,2,64,256]{4,3,0,2,1:T(8,128)(2,1)} %collective-permute-done.8), channel_id=1, source_target_pairs={{0,2},{2,4},{4,6},{6,8},{8,10},{10,12},{12,14},{14,16},{16,18},{18... | collective-permute-start | bytes 786440 | tf_op jit(solution)/shard_map/ppermute | solution.py:22
  842.2 17.7 %collective-permute-start.17 = (bf16[2,2,2,64,256]{4,3,0,2,1:T(8,128)(2,1)S(1)}, bf16[2,2,2,64,256]{4,3,0,2,1:T(8,128)(2,1)S(1)}, u32[]{:S(2)}, u32[]{:S(2)}) collective-permute-start(bf16[2,2,2,64,256]{4,3,0,2,1:T(8,128)(2,1)S(1)} %collective-permute-done.14), channel_id=1, source_target_pairs={{0,254},{2,0},{4,2},{6,4},{8,6},{10,8},{12,10},{14,12},{16,14},{18... | collective-permute-start | bytes 786440 | tf_op jit(solution)/shard_map/ppermute | solution.py:22
  1011.0 10.3 collective-permute-start.23
  1021.3 17.5 %collective-permute-start.24 = (bf16[2,2,2,64,128]{4,3,0,2,1:T(8,128)(2,1)S(1)}, bf16[2,2,2,64,128]{4,3,0,2,1:T(8,128)(2,1)S(1)}, u32[]{:S(2)}, u32[]{:S(2)}) collective-permute-start(bf16[2,2,2,64,128]{4,3,0,2,1:T(8,128)(2,1)S(1)} %collective-permute-done.23), channel_id=1, source_target_pairs={{0,16},{16,0},{2,18},{18,2},{4,20},{20,4},{6,22},{22,6},{8,24},{24... | collective-permute-start | bytes 393224 | tf_op jit(solution)/shard_map/ppermute | solution.py:17
  1038.7 24.1 %collective-permute-start.25 = (bf16[2,2,2,64,128]{4,3,0,2,1:T(8,128)(2,1)S(1)}, bf16[2,2,2,64,128]{4,3,0,2,1:T(8,128)(2,1)S(1)}, u32[]{:S(2)}, u32[]{:S(2)}) collective-permute-start(bf16[2,2,2,64,128]{4,3,0,2,1:T(8,128)(2,1)S(1)} %collective-permute-done.24), channel_id=1, source_target_pairs={{0,32},{32,0},{2,34},{34,2},{4,36},{36,4},{6,38},{38,6},{8,40},{40... | collective-permute-start | bytes 393224 | tf_op jit(solution)/shard_map/ppermute | solution.py:17
  1069.7 8.4 collective-permute-start.27
  (66 other events, 1590.5 us)
Sparse Core Ops, SparseCore 0:
  898.5 92.2 reduce-scatter.3
where the time goes:
time: 1100 us; the launch traced here: 1090 us
  blocking collectives  583 us (53%)
  waiting for transfers between devices  201 us (18%)
  starting transfers between devices  120 us (11%)
  matrix products  76.3 us (7%)
  other arithmetic  56 us (5%)
  local copies, waits for them, and re-layouts  35.4 us (3%)
  between operations  15.1 us (1%)
    psum x1, blocking collectives, per_device(): spread = lax.psum(spread, ('ka', 'isdf'))  583 us
    ppermute x16, waiting for transfers between devices, swapped(): return lax.ppermute(block, axis, route)  108 us
    unnamed x2, waiting for transfers between devices  92.5 us
    ppermute x16, starting transfers between devices, swapped(): return lax.ppermute(block, axis, route)  71.9 us
    dot_general x48, matrix products, single(): jnp.einsum(pattern, first, second, preferred_element_type=jnp.float32)  53.4 us
    ppermute x12, starting transfers between devices, shifted(): lax.ppermute(value, axis, [(i, (i + by) % size) for i in range(size)])  47.7 us
    mul x10, other arithmetic, accumulate(): screen_real * visit_real - screen_imag * visit_imag  23 us
    dot_general x10, matrix products, accumulate(): jnp.einsum('kw,wrmn->rkmn', selector[:, visitor], screened, preferred_ele...  22.4 us
  transfers between devices with their start and end apart: 29, of which 14 were waited for; matrix products, arithmetic and copies ran while one was open for 12% of the time, Pallas kernels for 0%

commit v1 on v0

--- a/solution.py
+++ b/solution.py
@@ -101,7 +101,12 @@
     )
     density = jnp.stack([rho_real, rho_imag], axis=1)
     spread = jnp.einsum("nm,brm->brn", coulomb, density, precision=HIGHEST)
-    spread = lax.psum(spread, ("ka", "isdf"))
+
+    def lead_the_bench(message):
+        w_next = lax.psum(message, axis_name="isdf")
+        return lax.psum(w_next, axis_name="ka")
+
+    spread = lead_the_bench(spread)
     potential = lax.dynamic_slice_in_dim(spread, isdf_index * mu_count, mu_count, 2)
     class_ids = jnp.arange(screened.shape[0], dtype=jnp.int32)
 

time: 1100 us -> 699 us (0.64)
  blocking collectives: 583 us -> 221 us
  waiting for transfers between devices: 201 us -> 165 us
    psum x1 -> x2, blocking collectives: 583 us -> 221 us  [the longest x1 215 us: lead_the_bench(): return lax.psum(w_next, axis_name='ka')]
    unnamed x2, waiting for transfers between devices: 92.5 us -> 56.5 us
  transfers between devices with their start and end apart: 29 -> 29, of which waited for: 14 -> 14; matrix products, arithmetic and copies ran while one was open for 12% -> 19% of each run, Pallas kernels for 0% -> 0%
where the time goes in v1:
time: 699 us; the launch traced here: 689 us
  blocking collectives  221 us (32%)
  waiting for transfers between devices  165 us (24%)
  starting transfers between devices  120 us (17%)
  matrix products  76.2 us (11%)
  other arithmetic  55.9 us (8%)
  local copies, waits for them, and re-layouts  35.4 us (5%)
  between operations  15.1 us (2%)
    psum x1, blocking collectives, lead_the_bench(): return lax.psum(w_next, axis_name='ka')  215 us
    ppermute x16, waiting for transfers between devices, swapped(): return lax.ppermute(block, axis, route)  108 us
    ppermute x16, starting transfers between devices, swapped(): return lax.ppermute(block, axis, route)  71.8 us
    unnamed x2, waiting for transfers between devices  56.5 us
    dot_general x48, matrix products, single(): jnp.einsum(pattern, first, second, preferred_element_type=jnp.float32)  53.4 us
    ppermute x12, starting transfers between devices, shifted(): lax.ppermute(value, axis, [(i, (i + by) % size) for i in range(size)])  47.7 us
    mul x10, other arithmetic, accumulate(): screen_real * visit_real - screen_imag * visit_imag  22.9 us
    dot_general x10, matrix products, accumulate(): jnp.einsum('kw,wrmn->rkmn', selector[:, visitor], screened, preferred_ele...  22.4 us
  transfers between devices with their start and end apart: 29, of which 14 were waited for; matrix products, arithmetic and copies ran while one was open for 19% of the time, Pallas kernels for 0%

profile of v1, /device:TPU:2, one launch (start us, length us, event | category | flops | bytes accessed | tf_op | source)
XLA Modules:
  0.0 688.6 jit_solution(6555879929286694897)
XLA Ops:
  8.6 10.8 %collective-permute-start.15 = (bf16[2,2,256,256]{3,2,1,0:T(8,128)(2,1)}, bf16[2,2,256,256]{3,2,1,0:T(8,128)(2,1)}, u32[]{:S(2)}, u32[]{:S(2)}) collective-permute-start(bf16[2,2,256,256]{3,2,1,0:T(8,128)(2,1)} %param.9), channel_id=1, source_target_pairs={{0,254},{2,0},{4,2},{6,4},{8,6},{10,8},{12,10},{14,12},{16,14},{18... | collective-permute-start | bytes 1572872 | tf_op jit(solution)/shard_map/ppermute | solution.py:22
  21.3 5.8 collective-permute-start.16
  78.0 6.5 collective-permute-done.2
  88.5 12.3 %collective-permute-done.3 = bf16[2,2,2,64,256]{4,3,0,2,1:T(8,128)(2,1)S(1)} collective-permute-done((bf16[2,2,2,64,256]{4,3,0,2,1:T(8,128)(2,1)S(1)}, bf16[2,2,2,64,256]{4,3,0,2,1:T(8,128)(2,1)S(1)}, u32[]{:S(2)}, u32[]{:S(2)}) %collective-permute-start.3) | collective-permute-done | bytes 262176 | tf_op jit(solution)/shard_map/ppermute | solution.py:17
  105.3 22.7 %collective-permute-done.4 = bf16[2,2,2,64,256]{4,3,0,2,1:T(8,128)(2,1)S(1)} collective-permute-done((bf16[2,2,2,64,256]{4,3,0,2,1:T(8,128)(2,1)S(1)}, bf16[2,2,2,64,256]{4,3,0,2,1:T(8,128)(2,1)S(1)}, u32[]{:S(2)}, u32[]{:S(2)}) %collective-permute-start.4) | collective-permute-done | bytes 262176 | tf_op jit(solution)/shard_map/ppermute | solution.py:17
  128.0 14.7 %collective-permute-start.5 = (bf16[2,2,2,64,256]{4,3,0,2,1:T(8,128)(2,1)S(1)}, bf16[2,2,2,64,256]{4,3,0,2,1:T(8,128)(2,1)S(1)}, u32[]{:S(2)}, u32[]{:S(2)}) collective-permute-start(bf16[2,2,2,64,256]{4,3,0,2,1:T(8,128)(2,1)S(1)} %collective-permute-done.4), channel_id=1, source_target_pairs={{0,32},{32,0},{2,34},{34,2},{4,36},{36,4},{6,38},{38,6},{8,40},{40... | collective-permute-start | bytes 786440 | tf_op jit(solution)/shard_map/ppermute | solution.py:17
  144.7 14.9 %collective-permute-done.5 = bf16[2,2,2,64,256]{4,3,0,2,1:T(8,128)(2,1)S(1)} collective-permute-done((bf16[2,2,2,64,256]{4,3,0,2,1:T(8,128)(2,1)S(1)}, bf16[2,2,2,64,256]{4,3,0,2,1:T(8,128)(2,1)S(1)}, u32[]{:S(2)}, u32[]{:S(2)}) %collective-permute-start.5) | collective-permute-done | bytes 262176 | tf_op jit(solution)/shard_map/ppermute | solution.py:17
  164.3 5.4 collective-permute-done.6
  200.1 5.8 collective-permute-start.19
  207.8 5.8 collective-permute-start.18
  225.0 6.6 psum.14
  231.6 214.8 %psum.15 = f32[2,2,512]{2,1,0:T(2,128)S(1)} all-reduce(f32[2,2,512]{2,1,0:T(2,128)S(1)} %psum.14), channel_id=1, replica_groups=mesh['pm'=2,'ka'=128,'isdf'=2] {'ka'}, use_global_device_ids=true, to_apply=%region_1.2 | all-reduce | flops 2048 | bytes 16384 | tf_op jit(solution)/shard_map/psum | solution.py:107
  480.6 5.2 collective-permute-start.17
  513.6 9.2 %add_convert_fusion = bf16[2,2,256,512]{3,2,0,1:T(8,128)(2,1)S(1)} fusion(f32[2,256,512]{2,1,0:T(8,128)} %get-tuple-element.46, f32[2,256,512]{2,1,0:T(8,128)S(1)} %copy-done.19, f32[2,256,512]{2,1,0:T(8,128)} %get-tuple-element.71, f32[2,256,512]{2,1,0:T(8,128)S(1)} %copy-done.18, f32[2,256,512]{2,1,0:T(8,128)} %get-tuple-element.45, ...), kind=kLoop, calls=%fused_computation | loop fusion | flops 20971520 | bytes 42991616 | tf_op jit(solution)/shard_map/convert_element_type | solution.py:161
  522.8 9.5 %add_convert_fusion.1 = bf16[2,2,256,512]{3,2,0,1:T(8,128)(2,1)S(1)} fusion(f32[2,256,512]{2,1,0:T(8,128)} %get-tuple-element.46, f32[2,256,512]{2,1,0:T(8,128)S(1)} %copy-done.19, f32[2,256,512]{2,1,0:T(8,128)} %get-tuple-element.71, f32[2,256,512]{2,1,0:T(8,128)S(1)} %copy-done.18, f32[2,256,512]{2,1,0:T(8,128)} %get-tuple-element.45, ...), kind=kLoop, calls=%fused_computation.1 | loop fusion | flops 20971520 | bytes 42991616 | tf_op jit(solution)/shard_map/convert_element_type | solution.py:160
  536.7 56.5 %reduce-scatter.4.cloned.1.call-done = bf16[128,512]{1,0:T(8,128)(2,1)} async-done(((bf16[256,512]{1,0:T(8,128)(2,1)}), bf16[128,512]{1,0:T(8,128)(2,1)}) %reduce-scatter.4.cloned.1.call-update) | async-done | bytes 131088
  598.0 4.6 collective-permute-done.20
  613.4 4.4 collective-permute-start.23
  617.8 5.9 collective-permute-done.23
  623.7 7.6 %collective-permute-start.24 = (bf16[2,2,2,64,128]{4,3,0,2,1:T(8,128)(2,1)S(1)}, bf16[2,2,2,64,128]{4,3,0,2,1:T(8,128)(2,1)S(1)}, u32[]{:S(2)}, u32[]{:S(2)}) collective-permute-start(bf16[2,2,2,64,128]{4,3,0,2,1:T(8,128)(2,1)S(1)} %collective-permute-done.23), channel_id=1, source_target_pairs={{0,16},{16,0},{2,18},{18,2},{4,20},{20,4},{6,22},{22,6},{8,24},{24... | collective-permute-start | bytes 393224 | tf_op jit(solution)/shard_map/ppermute | solution.py:17
  631.3 9.9 %collective-permute-done.24 = bf16[2,2,2,64,128]{4,3,0,2,1:T(8,128)(2,1)S(1)} collective-permute-done((bf16[2,2,2,64,128]{4,3,0,2,1:T(8,128)(2,1)S(1)}, bf16[2,2,2,64,128]{4,3,0,2,1:T(8,128)(2,1)S(1)}, u32[]{:S(2)}, u32[]{:S(2)}) %collective-permute-start.24) | collective-permute-done | bytes 131104 | tf_op jit(solution)/shard_map/ppermute | solution.py:17
  641.2 12.0 %collective-permute-start.25 = (bf16[2,2,2,64,128]{4,3,0,2,1:T(8,128)(2,1)S(1)}, bf16[2,2,2,64,128]{4,3,0,2,1:T(8,128)(2,1)S(1)}, u32[]{:S(2)}, u32[]{:S(2)}) collective-permute-start(bf16[2,2,2,64,128]{4,3,0,2,1:T(8,128)(2,1)S(1)} %collective-permute-done.24), channel_id=1, source_target_pairs={{0,32},{32,0},{2,34},{34,2},{4,36},{36,4},{6,38},{38,6},{8,40},{40... | collective-permute-start | bytes 393224 | tf_op jit(solution)/shard_map/ppermute | solution.py:17
  653.2 12.1 %collective-permute-done.25 = bf16[2,2,2,64,128]{4,3,0,2,1:T(8,128)(2,1)S(1)} collective-permute-done((bf16[2,2,2,64,128]{4,3,0,2,1:T(8,128)(2,1)S(1)}, bf16[2,2,2,64,128]{4,3,0,2,1:T(8,128)(2,1)S(1)}, u32[]{:S(2)}, u32[]{:S(2)}) %collective-permute-start.25) | collective-permute-done | bytes 131104 | tf_op jit(solution)/shard_map/ppermute | solution.py:17
  667.6 4.5 collective-permute-done.26
  (293 shorter events, 205.9 us)
Async XLA Ops:
  6.5 586.7 %reduce-scatter.4.cloned.1.call-start = ((), (), s32[]{:S(2)}) async-start(), calls=%async_computation.1 | async-start | bytes 393216
  6.5 199.3 %collective-permute-start.9 = (bf16[2,2,256,256]{3,2,1,0:T(8,128)(2,1)}, bf16[2,2,256,256]{3,2,1,0:T(8,128)(2,1)}, u32[]{:S(2)}, u32[]{:S(2)}) collective-permute-start(bf16[2,2,256,256]{3,2,1,0:T(8,128)(2,1)} %param.9), channel_id=1, source_target_pairs={{0,2},{2,4},{4,6},{6,8},{8,10},{10,12},{12,14},{14,16},{16,18},{18... | collective-permute-start | bytes 1572872 | tf_op jit(solution)/shard_map/ppermute | solution.py:22
  8.6 199.2 %collective-permute-start.15 = (bf16[2,2,256,256]{3,2,1,0:T(8,128)(2,1)}, bf16[2,2,256,256]{3,2,1,0:T(8,128)(2,1)}, u32[]{:S(2)}, u32[]{:S(2)}) collective-permute-start(bf16[2,2,256,256]{3,2,1,0:T(8,128)(2,1)} %param.9), channel_id=1, source_target_pairs={{0,254},{2,0},{4,2},{6,4},{8,6},{10,8},{12,10},{14,12},{16,14},{18... | collective-permute-start | bytes 1572872 | tf_op jit(solution)/shard_map/ppermute | solution.py:22
  19.4 178.6 %collective-permute-start.10 = (bf16[2,2,64,512]{3,2,1,0:T(8,128)(2,1)}, bf16[2,2,64,512]{3,2,1,0:T(8,128)(2,1)}, u32[]{:S(2)}, u32[]{:S(2)}) collective-permute-start(bf16[2,2,64,512]{3,2,1,0:T(8,128)(2,1)} %param.10), channel_id=1, source_target_pairs={{0,2},{2,4},{4,6},{6,8},{8,10},{10,12},{12,14},{14,16},{16,18},{18... | collective-permute-start | bytes 786440 | tf_op jit(solution)/shard_map/ppermute | solution.py:22
  21.3 178.7 %collective-permute-start.16 = (bf16[2,2,64,512]{3,2,1,0:T(8,128)(2,1)}, bf16[2,2,64,512]{3,2,1,0:T(8,128)(2,1)}, u32[]{:S(2)}, u32[]{:S(2)}) collective-permute-start(bf16[2,2,64,512]{3,2,1,0:T(8,128)(2,1)} %param.10), channel_id=1, source_target_pairs={{0,254},{2,0},{4,2},{6,4},{8,6},{10,8},{12,10},{14,12},{16,14},{18... | collective-permute-start | bytes 786440 | tf_op jit(solution)/shard_map/ppermute | solution.py:22
  28.1 41.6 %collective-permute-start = (bf16[2,2,2,64,256]{4,3,0,2,1:T(8,128)(2,1)S(1)}, bf16[2,2,2,64,256]{4,3,0,2,1:T(8,128)(2,1)S(1)}, u32[]{:S(2)}, u32[]{:S(2)}) collective-permute-start(bf16[2,2,2,64,256]{4,3,0,2,1:T(8,128)(2,1)S(1)} %bitcast.655), channel_id=1, source_target_pairs={{0,256},{256,0},{1,257},{257,1},{2,258},{258,2},{3,259},{259,3},{4... | collective-permute-start | bytes 786440 | tf_op jit(solution)/shard_map/ppermute | solution.py:17
  73.8 10.7 %collective-permute-start.2 = (bf16[2,2,2,64,256]{4,3,0,2,1:T(8,128)(2,1)S(1)}, bf16[2,2,2,64,256]{4,3,0,2,1:T(8,128)(2,1)S(1)}, u32[]{:S(2)}, u32[]{:S(2)}) collective-permute-start(bf16[2,2,2,64,256]{4,3,0,2,1:T(8,128)(2,1)S(1)} %collective-permute-done.1), channel_id=1, source_target_pairs={{0,4},{4,0},{2,6},{6,2},{8,12},{12,8},{10,14},{14,10},{16,20},{20,... | collective-permute-start | bytes 786440 | tf_op jit(solution)/shard_map/ppermute | solution.py:17
  84.6 16.3 %collective-permute-start.3 = (bf16[2,2,2,64,256]{4,3,0,2,1:T(8,128)(2,1)S(1)}, bf16[2,2,2,64,256]{4,3,0,2,1:T(8,128)(2,1)S(1)}, u32[]{:S(2)}, u32[]{:S(2)}) collective-permute-start(bf16[2,2,2,64,256]{4,3,0,2,1:T(8,128)(2,1)S(1)} %collective-permute-done.2), channel_id=1, source_target_pairs={{0,8},{8,0},{2,10},{10,2},{4,12},{12,4},{6,14},{14,6},{16,24},{24,... | collective-permute-start | bytes 786440 | tf_op jit(solution)/shard_map/ppermute | solution.py:17
  100.8 27.1 %collective-permute-start.4 = (bf16[2,2,2,64,256]{4,3,0,2,1:T(8,128)(2,1)S(1)}, bf16[2,2,2,64,256]{4,3,0,2,1:T(8,128)(2,1)S(1)}, u32[]{:S(2)}, u32[]{:S(2)}) collective-permute-start(bf16[2,2,2,64,256]{4,3,0,2,1:T(8,128)(2,1)S(1)} %collective-permute-done.3), channel_id=1, source_target_pairs={{0,16},{16,0},{2,18},{18,2},{4,20},{20,4},{6,22},{22,6},{8,24},{24... | collective-permute-start | bytes 786440 | tf_op jit(solution)/shard_map/ppermute | solution.py:17
  128.0 31.6 %collective-permute-start.5 = (bf16[2,2,2,64,256]{4,3,0,2,1:T(8,128)(2,1)S(1)}, bf16[2,2,2,64,256]{4,3,0,2,1:T(8,128)(2,1)S(1)}, u32[]{:S(2)}, u32[]{:S(2)}) collective-permute-start(bf16[2,2,2,64,256]{4,3,0,2,1:T(8,128)(2,1)S(1)} %collective-permute-done.4), channel_id=1, source_target_pairs={{0,32},{32,0},{2,34},{34,2},{4,36},{36,4},{6,38},{38,6},{8,40},{40... | collective-permute-start | bytes 786440 | tf_op jit(solution)/shard_map/ppermute | solution.py:17
  159.6 10.2 %collective-permute-start.6 = (bf16[2,2,2,64,256]{4,3,0,2,1:T(8,128)(2,1)S(1)}, bf16[2,2,2,64,256]{4,3,0,2,1:T(8,128)(2,1)}, u32[]{:S(2)}, u32[]{:S(2)}) collective-permute-start(bf16[2,2,2,64,256]{4,3,0,2,1:T(8,128)(2,1)S(1)} %collective-permute-done.5), channel_id=1, source_target_pairs={{0,64},{64,0},{2,66},{66,2},{4,68},{68,4},{6,70},{70,6},{8,72},{72... | collective-permute-start | bytes 786440 | tf_op jit(solution)/shard_map/ppermute | solution.py:17
  169.8 43.8 %collective-permute-start.7 = (bf16[2,2,2,64,256]{4,3,0,2,1:T(8,128)(2,1)}, bf16[2,2,2,64,256]{4,3,0,2,1:T(8,128)(2,1)}, u32[]{:S(2)}, u32[]{:S(2)}) collective-permute-start(bf16[2,2,2,64,256]{4,3,0,2,1:T(8,128)(2,1)} %collective-permute-done.6), channel_id=1, source_target_pairs={{0,128},{128,0},{2,130},{130,2},{4,132},{132,4},{6,134},{134,6},{8... | collective-permute-start | bytes 786440 | tf_op jit(solution)/shard_map/ppermute | solution.py:17
  198.0 292.4 %collective-permute-start.13 = (bf16[2,2,64,512]{3,2,1,0:T(8,128)(2,1)}, bf16[2,2,64,512]{3,2,1,0:T(8,128)(2,1)}, u32[]{:S(2)}, u32[]{:S(2)}) collective-permute-start(bf16[2,2,64,512]{3,2,1,0:T(8,128)(2,1)} %collective-permute-done.10), channel_id=1, source_target_pairs={{0,2},{2,4},{4,6},{6,8},{8,10},{10,12},{12,14},{14,16},{16,18},{18... | collective-permute-start | bytes 786440 | tf_op jit(solution)/shard_map/ppermute | solution.py:22
  200.1 302.8 %collective-permute-start.19 = (bf16[2,2,64,512]{3,2,1,0:T(8,128)(2,1)}, bf16[2,2,64,512]{3,2,1,0:T(8,128)(2,1)}, u32[]{:S(2)}, u32[]{:S(2)}) collective-permute-start(bf16[2,2,64,512]{3,2,1,0:T(8,128)(2,1)} %collective-permute-done.16), channel_id=1, source_target_pairs={{0,254},{2,0},{4,2},{6,4},{8,6},{10,8},{12,10},{14,12},{16,14},{18... | collective-permute-start | bytes 786440 | tf_op jit(solution)/shard_map/ppermute | solution.py:22
  205.9 274.8 %collective-permute-start.12 = (bf16[2,2,256,256]{3,2,1,0:T(8,128)(2,1)}, bf16[2,2,256,256]{3,2,1,0:T(8,128)(2,1)}, u32[]{:S(2)}, u32[]{:S(2)}) collective-permute-start(bf16[2,2,256,256]{3,2,1,0:T(8,128)(2,1)} %collective-permute-done.9), channel_id=1, source_target_pairs={{0,2},{2,4},{4,6},{6,8},{8,10},{10,12},{12,14},{14,16},{16,18},{18... | collective-permute-start | bytes 1572872 | tf_op jit(solution)/shard_map/ppermute | solution.py:22
  207.8 290.4 %collective-permute-start.18 = (bf16[2,2,256,256]{3,2,1,0:T(8,128)(2,1)}, bf16[2,2,256,256]{3,2,1,0:T(8,128)(2,1)}, u32[]{:S(2)}, u32[]{:S(2)}) collective-permute-start(bf16[2,2,256,256]{3,2,1,0:T(8,128)(2,1)} %collective-permute-done.15), channel_id=1, source_target_pairs={{0,254},{2,0},{4,2},{6,4},{8,6},{10,8},{12,10},{14,12},{16,14},{18... | collective-permute-start | bytes 1572872 | tf_op jit(solution)/shard_map/ppermute | solution.py:22
  217.8 233.1 %collective-permute-start.8 = (bf16[2,2,2,64,256]{4,3,0,2,1:T(8,128)(2,1)}, bf16[2,2,2,64,256]{4,3,0,2,1:T(8,128)(2,1)}, u32[]{:S(2)}, u32[]{:S(2)}) collective-permute-start(bf16[2,2,2,64,256]{4,3,0,2,1:T(8,128)(2,1)} %fusion.89), channel_id=1, source_target_pairs={{0,2},{2,4},{4,6},{6,8},{8,10},{10,12},{12,14},{14,16},{16,18},{18... | collective-permute-start | bytes 786440 | tf_op jit(solution)/shard_map/ppermute | solution.py:22
  450.9 14.6 %collective-permute-start.14 = (bf16[2,2,2,64,256]{4,3,0,2,1:T(8,128)(2,1)}, bf16[2,2,2,64,256]{4,3,0,2,1:T(8,128)(2,1)S(1)}, u32[]{:S(2)}, u32[]{:S(2)}) collective-permute-start(bf16[2,2,2,64,256]{4,3,0,2,1:T(8,128)(2,1)} %fusion.89), channel_id=1, source_target_pairs={{0,254},{2,0},{4,2},{6,4},{8,6},{10,8},{12,10},{14,12},{16,14},{18... | collective-permute-start | bytes 786440 | tf_op jit(solution)/shard_map/ppermute | solution.py:22
  465.6 20.3 %collective-permute-start.11 = (bf16[2,2,2,64,256]{4,3,0,2,1:T(8,128)(2,1)}, bf16[2,2,2,64,256]{4,3,0,2,1:T(8,128)(2,1)S(1)}, u32[]{:S(2)}, u32[]{:S(2)}) collective-permute-start(bf16[2,2,2,64,256]{4,3,0,2,1:T(8,128)(2,1)} %collective-permute-done.8), channel_id=1, source_target_pairs={{0,2},{2,4},{4,6},{6,8},{8,10},{10,12},{12,14},{14,16},{16,18},{18... | collective-permute-start | bytes 786440 | tf_op jit(solution)/shard_map/ppermute | solution.py:22
  480.6 17.6 %collective-permute-start.17 = (bf16[2,2,2,64,256]{4,3,0,2,1:T(8,128)(2,1)S(1)}, bf16[2,2,2,64,256]{4,3,0,2,1:T(8,128)(2,1)S(1)}, u32[]{:S(2)}, u32[]{:S(2)}) collective-permute-start(bf16[2,2,2,64,256]{4,3,0,2,1:T(8,128)(2,1)S(1)} %collective-permute-done.14), channel_id=1, source_target_pairs={{0,254},{2,0},{4,2},{6,4},{8,6},{10,8},{12,10},{14,12},{16,14},{18... | collective-permute-start | bytes 786440 | tf_op jit(solution)/shard_map/ppermute | solution.py:22
  613.4 10.3 %collective-permute-start.23 = (bf16[2,2,2,64,128]{4,3,0,2,1:T(8,128)(2,1)S(1)}, bf16[2,2,2,64,128]{4,3,0,2,1:T(8,128)(2,1)S(1)}, u32[]{:S(2)}, u32[]{:S(2)}) collective-permute-start(bf16[2,2,2,64,128]{4,3,0,2,1:T(8,128)(2,1)S(1)} %collective-permute-done.22), channel_id=1, source_target_pairs={{0,8},{8,0},{2,10},{10,2},{4,12},{12,4},{6,14},{14,6},{16,24},{24,... | collective-permute-start | bytes 393224 | tf_op jit(solution)/shard_map/ppermute | solution.py:17
  623.7 17.5 %collective-permute-start.24 = (bf16[2,2,2,64,128]{4,3,0,2,1:T(8,128)(2,1)S(1)}, bf16[2,2,2,64,128]{4,3,0,2,1:T(8,128)(2,1)S(1)}, u32[]{:S(2)}, u32[]{:S(2)}) collective-permute-start(bf16[2,2,2,64,128]{4,3,0,2,1:T(8,128)(2,1)S(1)} %collective-permute-done.23), channel_id=1, source_target_pairs={{0,16},{16,0},{2,18},{18,2},{4,20},{20,4},{6,22},{22,6},{8,24},{24... | collective-permute-start | bytes 393224 | tf_op jit(solution)/shard_map/ppermute | solution.py:17
  641.2 24.1 %collective-permute-start.25 = (bf16[2,2,2,64,128]{4,3,0,2,1:T(8,128)(2,1)S(1)}, bf16[2,2,2,64,128]{4,3,0,2,1:T(8,128)(2,1)S(1)}, u32[]{:S(2)}, u32[]{:S(2)}) collective-permute-start(bf16[2,2,2,64,128]{4,3,0,2,1:T(8,128)(2,1)S(1)} %collective-permute-done.24), channel_id=1, source_target_pairs={{0,32},{32,0},{2,34},{34,2},{4,36},{36,4},{6,38},{38,6},{8,40},{40... | collective-permute-start | bytes 393224 | tf_op jit(solution)/shard_map/ppermute | solution.py:17
  672.1 8.4 %collective-permute-start.27 = (bf16[2,2,2,64,128]{4,3,0,2,1:T(8,128)(2,1)S(1)}, bf16[2,2,2,64,128]{4,3,0,2,1:T(8,128)(2,1)S(1)}, u32[]{:S(2)}, u32[]{:S(2)}) collective-permute-start(bf16[2,2,2,64,128]{4,3,0,2,1:T(8,128)(2,1)S(1)} %collective-permute-done.26), channel_id=1, source_target_pairs={{0,128},{128,0},{2,130},{130,2},{4,132},{132,4},{6,134},{134,6},{8... | collective-permute-start | bytes 393224 | tf_op jit(solution)/shard_map/ppermute | solution.py:17
  (66 other events, 1156.9 us)
Sparse Core Ops, SparseCore 0:
  536.9 56.3 reduce-scatter.3
